TPU v7x, 32 devices: a whole 2x2x4 slice. The times are simulated.
32 devices in a mesh: row: 4 (over z), col: 8 (over y, x, core).
Axes of the slice: x: 2, y: 2, z: 4, core: 2. Of those that a mesh axis runs over, the one named last changes fastest.
Arguments:
- tokens: bfloat16 [64, 8192], P('row', 'col'), may hold values from -6 to 6
- gate_weight: bfloat16 [8192, 26624], P('col', 'row'), may hold values from -0.0625 to 0.0625
- up_weight: bfloat16 [8192, 26624], P('col', 'row'), may hold values from -0.0625 to 0.0625
- down_weight: bfloat16 [26624, 8192], P('row', 'col'), may hold values from -0.0390625 to 0.0390625
- gate_tangent: bfloat16 [8192, 26624], P('col', 'row'), may hold values from -0.0625 to 0.0625
- up_tangent: bfloat16 [8192, 26624], P('col', 'row'), may hold values from -0.0625 to 0.0625
Outputs:
- gate_product: bfloat16 [8192, 26624], P('col', 'row')
- up_product: bfloat16 [8192, 26624], P('col', 'row')
All inputs are finite; a program needn't handle non-finite values.
Results may differ from a plain program's by a relative error of at most 0.0085.
Values may be sent and summed in bfloat16 or wider, within the bound.
A program may use at most 192 MiB of HBM per device.

v0:
```python
import jax
import jax.numpy as jnp
from jax import lax
from jax.sharding import PartitionSpec as P


def matmul(left, right):
    return jnp.dot(left, right, preferred_element_type=jnp.float32)


def transposed(left, right):
    return lax.dot_general(
        left, right, (((0,), (0,)), ((), ())), preferred_element_type=jnp.float32
    )


def against_rows(left, right):
    return lax.dot_general(
        left, right, (((1,), (1,)), ((), ())), preferred_element_type=jnp.float32
    )


def silu_terms(gate_sum):
    sigmoid_val = jax.nn.sigmoid(gate_sum)
    return (gate_sum * sigmoid_val, sigmoid_val * (1.0 + gate_sum * (1.0 - sigmoid_val)))


def tangent_hidden(activated, slopes, up_sum, gate_dir, up_dir):
    return (slopes * gate_dir * up_sum + activated * up_dir).astype(jnp.bfloat16)


def cotangents(back_sum, up_sum, activated, slopes):
    gate_cot = (back_sum * up_sum * slopes).astype(jnp.bfloat16)
    up_cot = (back_sum * activated).astype(jnp.bfloat16)
    return (gate_cot, up_cot)


def body(tokens, gate_weight, up_weight, down_weight, gate_tangent, up_tangent):
    gathered = lax.all_gather(tokens, "row", axis=0, tiled=True)
    total_rows = gathered.shape[0]
    out_scale = float(total_rows) ** (-0.5)
    gate_sum, up_sum, gate_dir, up_dir = lax.psum(
        (
            matmul(gathered, gate_weight),
            matmul(gathered, up_weight),
            matmul(gathered, gate_tangent),
            matmul(gathered, up_tangent),
        ),
        "col",
    )
    activated, slopes = silu_terms(gate_sum)
    hidden_dir = tangent_hidden(activated, slopes, up_sum, gate_dir, up_dir)
    output_part = matmul(hidden_dir, down_weight)
    output_dir = (lax.psum(output_part, "row") * out_scale).astype(jnp.bfloat16)
    back_sum = lax.psum(against_rows(output_dir, down_weight), "col")
    gate_cot, up_cot = cotangents(back_sum, up_sum, activated, slopes)
    gate_grad = transposed(gathered, gate_cot)
    up_grad = transposed(gathered, up_cot)
    return (gate_grad.astype(jnp.bfloat16), up_grad.astype(jnp.bfloat16))


def solution(mesh):
    placed = (
        P("row", "col"),
        P("col", "row"),
        P("col", "row"),
        P("row", "col"),
        P("col", "row"),
        P("col", "row"),
    )
    return jax.shard_map(
        body,
        mesh=mesh,
        in_specs=placed,
        out_specs=(P("col", "row"), P("col", "row")),
        check_vma=False,
    )
```

profile of v0, /device:TPU:0, one launch (start us, length us, event | category | flops | bytes accessed | tf_op | source)
XLA Modules:
  0.0 331.8 jit_solution(806123862616098601)
XLA Ops:
  7.2 0.0 all-reduce.9.cloned.1.call-start
  7.2 15.3 %all_gather.3 = bf16[64,1024]{1,0:T(8,128)(2,1)S(1)} all-gather(bf16[16,1024]{1,0:T(8,128)(2,1)} %param.6), channel_id=1, replica_groups=mesh['row'=4,'col'=8] {'row'}, dimensions={0}, use_global_device_ids=true | all-gather | bytes 163840 | tf_op jit(solution)/shard_map/all_gather | solution.py:39
  22.5 8.7 %fusion.12 = f32[64,6656]{1,0:T(8,128)} fusion(bf16[64,1024]{1,0:T(8,128)(2,1)S(1)} %all_gather.3, bf16[1024,6656]{1,0:T(8,128)(2,1)} %param.11), kind=kOutput, calls=%fused_computation.18 | convolution fusion | flops 872415232 | bytes 15466496 | tf_op jit(solution)/shard_map/dot_general | solution.py:8
  31.2 0.7 copy-done.1
  31.9 3.6 %fusion.11 = f32[64,6656]{1,0:T(8,128)} fusion(bf16[64,1024]{1,0:T(8,128)(2,1)S(1)} %all_gather.3, bf16[1024,6656]{1,0:T(8,128)(2,1)S(1)} %copy-done.1), kind=kOutput, calls=%fused_computation.17 | convolution fusion | flops 872415232 | bytes 15466496 | tf_op jit(solution)/shard_map/dot_general | solution.py:8
  35.5 1.8 copy-done.2
  37.3 3.7 %fusion.10 = f32[64,6656]{1,0:T(8,128)} fusion(bf16[64,1024]{1,0:T(8,128)(2,1)S(1)} %all_gather.3, bf16[1024,6656]{1,0:T(8,128)(2,1)S(1)} %copy-done.2), kind=kOutput, calls=%fused_computation.16 | convolution fusion | flops 872415232 | bytes 15466496 | tf_op jit(solution)/shard_map/dot_general | solution.py:8
  41.0 1.8 copy-done.3
  42.8 3.7 %fusion.9 = f32[64,6656]{1,0:T(8,128)} fusion(bf16[64,1024]{1,0:T(8,128)(2,1)S(1)} %all_gather.3, bf16[1024,6656]{1,0:T(8,128)(2,1)S(1)} %copy-done.3), kind=kOutput, calls=%fused_computation.15 | convolution fusion | flops 872415232 | bytes 15466496 | tf_op jit(solution)/shard_map/dot_general | solution.py:8
  46.5 0.0 all-reduce.9.cloned.1.call-update
  46.6 0.0 all-reduce.5.cloned.1.call-start
  46.6 112.0 %all-reduce.9.cloned.1.call-done = (f32[64,6656]{1,0:T(8,128)}, f32[64,6656]{1,0:T(8,128)}, f32[64,6656]{1,0:T(8,128)}, f32[64,6656]{1,0:T(8,128)}) async-done(((f32[64,6656]{1,0:T(8,128)}, f32[64,6656]{1,0:T(8,128)}, f32[64,6656]{1,0:T(8,128)}, f32[64,6656]{1,0:T(8,128)}), (f32[64,6656]{1,0:T(8,128)}, f32[64,6656]{1,0:T(8,128)}, f32[64,6656]{1,0:T(8,128)}, ...) | async-done | bytes 6815760 | tf_op jit(solution)/shard_map/psum | solution.py:42
  158.6 10.6 %fusion.1 = f32[64,1024]{1,0:T(8,128)} fusion(bf16[6656,1024]{1,0:T(8,128)(2,1)} %param.9, f32[64,6656]{1,0:T(8,128)} %get-tuple-element.4, f32[64,6656]{1,0:T(8,128)} %get-tuple-element.5, f32[64,6656]{1,0:T(8,128)} %get-tuple-element.6, f32[64,6656]{1,0:T(8,128)} %get-tuple-element.7), kind=kOutput, calls=%fused_computation.8 | convolution fusion | flops 877953024 | bytes 20709376 | tf_op jit(solution)/shard_map/dot_general | solution.py:8
  169.2 0.0 all-reduce.5.cloned.1.call-update
  169.2 0.2 all-reduce.7.cloned.1.call-start
  169.5 35.3 %all-reduce.5.cloned.1.call-done = f32[64,1024]{1,0:T(8,128)} async-done(((f32[64,1024]{1,0:T(8,128)}), f32[64,1024]{1,0:T(8,128)}) %all-reduce.5.cloned.1.call-update) | async-done | bytes 262160 | tf_op jit(solution)/shard_map/psum | solution.py:54
  204.8 10.5 %fusion.4 = f32[64,6656]{1,0:T(8,128)} fusion(bf16[6656,1024]{1,0:T(8,128)(2,1)} %param.9, f32[64,1024]{1,0:T(8,128)} %all-reduce.5.cloned.1.call-done), kind=kOutput, calls=%fused_computation.10 | convolution fusion | flops 872546304 | bytes 15597568 | tf_op jit(solution)/shard_map/dot_general | solution.py:18
  215.3 0.0 all-reduce.7.cloned.1.call-update
  215.3 59.4 %all-reduce.7.cloned.1.call-done = f32[64,6656]{1,0:T(8,128)} async-done(((f32[64,6656]{1,0:T(8,128)}), f32[64,6656]{1,0:T(8,128)}) %all-reduce.7.cloned.1.call-update) | async-done | bytes 1703952 | tf_op jit(solution)/shard_map/psum | solution.py:55
  274.8 0.0 copy-done
  274.8 8.6 %convert_bitcast_fusion.1 = bf16[1024,6656]{0,1:T(8,128)(2,1)} fusion(bf16[64,1024]{1,0:T(8,128)(2,1)S(1)} %all_gather.3, f32[64,6656]{1,0:T(8,128)} %all-reduce.7.cloned.1.call-done, f32[64,6656]{1,0:T(8,128)S(1)} %copy-done.4, f32[64,6656]{1,0:T(8,128)S(1)} %copy-done), kind=kOutput, calls=%fused_computation.1 | convolution fusion | flops 883490816 | bytes 18874368 | tf_op jit(solution)/shard_map/dot_general | solution.py:12
  283.4 17.6 %copy.8 = bf16[1024,6656]{1,0:T(8,128)(2,1)} copy(bf16[1024,6656]{0,1:T(8,128)(2,1)} %convert_bitcast_fusion.1) | data formatting | bytes 27262976
  300.9 6.9 %convert_bitcast_fusion = bf16[1024,6656]{0,1:T(8,128)(2,1)} fusion(bf16[64,1024]{1,0:T(8,128)(2,1)S(1)} %all_gather.3, f32[64,6656]{1,0:T(8,128)S(1)} %copy-done.5, f32[64,6656]{1,0:T(8,128)S(1)} %copy-done), kind=kOutput, calls=%fused_computation | convolution fusion | flops 881786880 | bytes 17170432 | tf_op jit(solution)/shard_map/dot_general | solution.py:12
  307.8 17.4 %copy.9 = bf16[1024,6656]{1,0:T(8,128)(2,1)} copy(bf16[1024,6656]{0,1:T(8,128)(2,1)} %convert_bitcast_fusion) | data formatting | bytes 27262976
  (8 shorter events, 0.0 us)
Async XLA Ops:
  7.2 151.4 %all-reduce.9.cloned.1.call-start = ((), (), s32[]{:S(2)}) async-start(), calls=%async_computation.2 | async-start | bytes 13631488 | tf_op jit(solution)/shard_map/psum | solution.py:42
  22.5 9.4 %copy-start.1 = (bf16[1024,6656]{1,0:T(8,128)(2,1)S(1)}, bf16[1024,6656]{1,0:T(8,128)(2,1)}, u32[]{:S(2)}) copy-start(bf16[1024,6656]{1,0:T(8,128)(2,1)} %param.8) | copy-start | bytes 40894468
  31.9 5.5 %copy-start.2 = (bf16[1024,6656]{1,0:T(8,128)(2,1)S(1)}, bf16[1024,6656]{1,0:T(8,128)(2,1)}, u32[]{:S(2)}) copy-start(bf16[1024,6656]{1,0:T(8,128)(2,1)} %param.10) | copy-start | bytes 40894468
  37.3 5.5 %copy-start.3 = (bf16[1024,6656]{1,0:T(8,128)(2,1)S(1)}, bf16[1024,6656]{1,0:T(8,128)(2,1)}, u32[]{:S(2)}) copy-start(bf16[1024,6656]{1,0:T(8,128)(2,1)} %param.7) | copy-start | bytes 40894468
  46.6 158.2 %all-reduce.5.cloned.1.call-start = ((), (), s32[]{:S(2)}) async-start(), calls=%async_computation | async-start | bytes 524288 | tf_op jit(solution)/shard_map/psum | solution.py:54
  169.2 105.5 %all-reduce.7.cloned.1.call-start = ((), (), s32[]{:S(2)}) async-start(), calls=%async_computation.1 | async-start | bytes 3407872 | tf_op jit(solution)/shard_map/psum | solution.py:55
  204.8 70.0 %copy-start.4 = (f32[64,6656]{1,0:T(8,128)S(1)}, f32[64,6656]{1,0:T(8,128)}, u32[]{:S(2)}) copy-start(f32[64,6656]{1,0:T(8,128)} %get-tuple-element.5) | copy-start | bytes 5111812
  215.3 59.5 %copy-start = (f32[64,6656]{1,0:T(8,128)S(1)}, f32[64,6656]{1,0:T(8,128)}, u32[]{:S(2)}) copy-start(f32[64,6656]{1,0:T(8,128)} %get-tuple-element.7) | copy-start | bytes 5111812
  283.4 17.6 %copy-start.5 = (f32[64,6656]{1,0:T(8,128)S(1)}, f32[64,6656]{1,0:T(8,128)}, u32[]{:S(2)}) copy-start(f32[64,6656]{1,0:T(8,128)} %all-reduce.7.cloned.1.call-done) | copy-start | bytes 5111812
Sparse Core Ops, SparseCore 0:
  46.7 111.8 all-reduce.8
  169.4 35.3 all-reduce.4
  215.5 59.2 all-reduce.6
where the time goes:
time: 333 us; the launch traced here: 332 us
  waiting for transfers between devices  207 us (62%)
  matrix products  56.3 us (17%)
  local copies, waits for them, and re-layouts  39.3 us (12%)
  blocking collectives  15.3 us (5%)
  between operations  13.8 us (4%)
    psum x1, waiting for transfers between devices, body(): lax.psum((matmul(gathered, gate_weight), matmul(gathered, up_weight), mat...  112 us
    psum x1, waiting for transfers between devices, body(): back_sum = lax.psum(against_rows(output_dir, down_weight), 'col')  59.4 us
    unnamed x14, local copies, waits for them, and re-layouts  39.3 us
    psum x1, waiting for transfers between devices, body(): output_dir = (lax.psum(output_part, 'row') * out_scale).astype(jnp.bfloat16)  35.3 us
    dot_general x5, matrix products, matmul(): return jnp.dot(left, right, preferred_element_type=jnp.float32)  30.4 us
    dot_general x2, matrix products, transposed(): lax.dot_general(left, right, (((0,), (0,)), ((), ())), preferred_element_...  15.4 us
    all_gather x1, blocking collectives, body(): gathered = lax.all_gather(tokens, 'row', axis=0, tiled=True)  15.3 us
    dot_general x1, matrix products, against_rows(): lax.dot_general(left, right, (((1,), (1,)), ((), ())), preferred_element_...  10.5 us
  transfers between devices with their start and end apart: 3, of which 3 were waited for; matrix products, arithmetic and copies ran while one was open for 0% of the time, Pallas kernels for 0%

commit v1 on v0

v1 whole, which is shorter than its diff:
```python
import functools

import jax
import jax.numpy as jnp
from jax import lax
from jax.experimental import pallas as pl
from jax.experimental.pallas import tpu as pltpu
from jax.sharding import PartitionSpec as P

BF = jnp.bfloat16
F32 = jnp.float32
MESH = pl.DeviceIdType.MESH
SLOTS = 3
CHUNKS = 13
LAG = 1


def curvature_kernel(n, nr, k, names, *refs):
    r = dict(zip(names, refs))
    tokens, weights, down = r["tokens"], [r["gw"], r["uw"], r["gt"], r["ut"]], r["dw"]
    x, w, dn = r["x"], r["w"], r["dn"]
    total, depth = x.shape
    chunk = w.shape[-1]
    half = chunk // 2
    tpo = total // n
    rpr = total // nr
    scale = float(total) ** (-0.5)
    row, me = lax.axis_index("row"), lax.axis_index("col")

    def stride(l, c):
        a = 1 << l
        b = 1 if l == 0 else 1 << (k - l)
        return a if a == b else a + (b - a) * lax.rem(c, 2)

    def bit(l, c):
        return lax.rem(lax.div(me, stride(l, c)), 2)

    def partner(l, c):
        return me + (1 - 2 * bit(l, c)) * stride(l, c)

    def place(c):
        total_place = 0
        for l in range(k):
            total_place = total_place + bit(l, c) * (1 << (k - 1 - l))
        return total_place

    def weight_copy(c, j):
        slot = lax.rem(c, SLOTS)
        cols = pl.ds(pl.multiple_of(c * chunk, chunk), chunk)
        return pltpu.make_async_copy(weights[j].at[:, cols], w.at[slot, j], r["wsem"].at[slot, j])

    def down_copy(c):
        rows = pl.ds(pl.multiple_of(c * chunk, chunk), chunk)
        return pltpu.make_async_copy(down.at[rows], dn.at[c], r["dsem"].at[c])

    def rs_copy(tag, l, c):
        return pltpu.make_async_remote_copy(
            src_ref=r[tag + "s%d" % l].at[c],
            dst_ref=r[tag + "r%d" % l].at[c],
            send_sem=r[tag + "ss"].at[l, c],
            recv_sem=r[tag + "rs"].at[l, c],
            device_id=(row, partner(l, c)),
            device_id_type=MESH,
        )

    def ag_copy(buf, tag, l, c, arriving=False):
        size = 1 << (k - 1 - l)
        base = lax.div(place(c), size) * size
        if arriving:
            base = base + (1 - 2 * bit(l, c)) * size
        part = r[buf].at[c, pl.ds(base, size)]
        return pltpu.make_async_remote_copy(
            src_ref=part,
            dst_ref=part,
            send_sem=r[tag + "sa"].at[l, c],
            recv_sem=r[tag + "ra"].at[l, c],
            device_id=(row, partner(l, c)),
            device_id_type=MESH,
        )

    def ag_wait(buf, tag, l, c):
        ag_copy(buf, tag, l, c).wait_send()
        ag_copy(buf, tag, l, c, arriving=True).wait_recv()

    def rs_step(tag, l, c):
        rs_copy(tag, l, c).wait()
        kept, got = r[tag + "k%d" % l], r[tag + "r%d" % l]
        m = kept.shape[1] // 2
        b = bit(l + 1, c)
        other, mine = pl.ds((1 - b) * m, m), pl.ds(b * m, m)
        r[tag + "s%d" % (l + 1)][c] = (kept[c, other] + got[c, other].astype(F32)).astype(BF)
        rs_copy(tag, l + 1, c).start()
        r[tag + "k%d" % (l + 1)][c] = kept[c, mine] + got[c, mine].astype(F32)

    def rs_last(tag, c):
        rs_copy(tag, k - 1, c).wait()
        return r[tag + "k%d" % (k - 1)][c, 0] + r[tag + "r%d" % (k - 1)][c, 0].astype(F32)

    def peer(d):
        return lax.rem(row + d, nr)

    def source(d):
        return lax.rem(row + nr - d, nr)

    def rows_of(q):
        return pl.ds(pl.multiple_of(q * rpr, rpr), rpr)

    def row_copy(src, dst, tag, d):
        return pltpu.make_async_remote_copy(
            src_ref=src,
            dst_ref=dst,
            send_sem=r[tag + "s"].at[d],
            recv_sem=r[tag + "r"].at[d],
            device_id=(peer(d), me),
            device_id_type=MESH,
        )

    def token_send(d):
        return row_copy(tokens, x.at[rows_of(row)], "t", d)

    def token_arrival(d):
        return row_copy(tokens, x.at[rows_of(source(d))], "t", d)

    own_tokens = pltpu.make_async_copy(tokens, x.at[rows_of(row)], r["osem"])
    own_tokens.start()
    for c in range(SLOTS):
        for j in range(4):
            weight_copy(c, j).start()

    barrier = pltpu.get_barrier_semaphore()
    for l in range(k):
        pl.semaphore_signal(barrier, inc=1, device_id=(row, partner(l, 0)), device_id_type=MESH)
    for d in range(1, nr):
        pl.semaphore_signal(barrier, inc=1, device_id=(peer(d), me), device_id_type=MESH)
    pl.semaphore_wait(barrier, k + nr - 1)

    for d in range(1, nr):
        token_send(d).start()
    own_tokens.wait()
    for d in range(1, nr):
        token_send(d).wait_send()
        token_arrival(d).wait_recv()
    r["acc"][...] = jnp.zeros_like(r["acc"])

    def project(c):
        slot = lax.rem(c, SLOTS)
        pf = r["pf"]
        for j in range(4):
            weight_copy(c, j).wait()
            pf[j] = jnp.dot(x[...], w[slot, j], preferred_element_type=F32)

        @pl.when(c + SLOTS < CHUNKS)
        def _():
            for j in range(4):
                weight_copy(c + SLOTS, j).start()

        down_copy(c).start()
        b = bit(0, c)
        span = total // 2
        for p in range(n // 2):
            rows = pl.ds(pl.multiple_of((1 - b) * span + p * tpo, tpo), tpo)
            r["hs0"][c, p] = jnp.concatenate([pf[j, rows] for j in range(4)], axis=0).astype(BF)
        rs_copy("h", 0, c).start()
        for p in range(n // 2):
            rows = pl.ds(pl.multiple_of(b * span + p * tpo, tpo), tpo)
            r["hk0"][c, p] = jnp.concatenate([pf[j, rows] for j in range(4)], axis=0)

    def hidden(c):
        sums = rs_last("h", c)
        gate_sum, up_sum, gate_dir, up_dir = (sums[j * tpo:(j + 1) * tpo] for j in range(4))
        sig = jax.nn.sigmoid(gate_sum)
        activated = gate_sum * sig
        slopes = sig * (1.0 + gate_sum * (1.0 - sig))
        slope_up = slopes * up_sum
        r["cg"][c] = slope_up
        r["cu"][c] = activated
        hid = slope_up * gate_dir + activated * up_dir
        r["h"][c, place(c)] = jnp.concatenate([hid[:, :half], hid[:, half:]], axis=0).astype(BF)
        ag_copy("h", "h", k - 1, c).start()

    def ag_step(buf, tag, l, c):
        ag_wait(buf, tag, l, c)
        ag_copy(buf, tag, l - 1, c).start()

    def down_part(c):
        ag_wait("h", "h", 0, c)
        down_copy(c).wait()
        got = r["h"][c].astype(F32)
        rows = [jnp.concatenate([got[p, :tpo], got[p, tpo:]], axis=1) for p in range(n)]
        hid = jnp.concatenate(rows, axis=0).astype(BF)
        r["acc"][...] += jnp.dot(hid, dn[c], preferred_element_type=F32)

    def run(stages):
        def step(i, carry):
            for s, stage in enumerate(stages):
                c = i - s * LAG

                @pl.when(jnp.logical_and(c >= 0, c < CHUNKS))
                def _():
                    stage(c)
            return carry

        lax.fori_loop(0, CHUNKS + LAG * (len(stages) - 1), step, 0)

    run(
        [project]
        + [functools.partial(rs_step, "h", l) for l in range(k - 1)]
        + [hidden]
        + [functools.partial(ag_step, "h", "h", l) for l in range(k - 1, 0, -1)]
        + [down_part]
    )

    acc, q, qs, o = r["acc"], r["q"], r["qs"], r["o"]

    def part_send(d):
        return row_copy(qs.at[d], q.at[d], "p", d)

    def out_send(d):
        return row_copy(o.at[rows_of(row)], o.at[rows_of(row)], "o", d)

    def out_arrival(d):
        return row_copy(o.at[rows_of(source(d))], o.at[rows_of(source(d))], "o", d)

    for d in range(1, nr):
        qs[d] = acc[rows_of(peer(d))].astype(BF)
        part_send(d).start()
    out = acc[rows_of(row)]
    for d in range(1, nr):
        part_send(d).wait()
        out = out + q[d].astype(F32)
    o[rows_of(row)] = (out * scale).astype(BF)
    for d in range(1, nr):
        out_send(d).start()
    r["tt"][...] = jnp.transpose(x[...].astype(F32)).astype(BF)
    for d in range(1, nr):
        out_send(d).wait_send()
        out_arrival(d).wait_recv()

    def back(c):
        pb = r["pb"]
        pb[...] = lax.dot_general(
            o[...], dn[c], (((1,), (1,)), ((), ())), preferred_element_type=F32
        )
        b = bit(0, c)
        span = total // 2
        for p in range(n // 2):
            rows = pl.ds(pl.multiple_of((1 - b) * span + p * tpo, tpo), tpo)
            r["bs0"][c, p] = jnp.concatenate([pb[rows, :half], pb[rows, half:]], axis=0).astype(BF)
        rs_copy("b", 0, c).start()
        for p in range(n // 2):
            rows = pl.ds(pl.multiple_of(b * span + p * tpo, tpo), tpo)
            r["bk0"][c, p] = jnp.concatenate([pb[rows, :half], pb[rows, half:]], axis=0)

    def cots(c):
        sums = rs_last("b", c)
        back_sum = jnp.concatenate([sums[:tpo], sums[tpo:]], axis=1)
        both = [back_sum * r["cg"][c], back_sum * r["cu"][c]]
        r["g"][c, place(c)] = jnp.concatenate(both, axis=0).astype(BF)
        ag_copy("g", "b", k - 1, c).start()

    def spread(c):
        ag_wait("g", "b", 0, c)
        got = r["g"][c].astype(F32)
        r["gc"][c] = jnp.concatenate([got[p, :tpo] for p in range(n)], axis=0).astype(BF)
        r["uc"][c] = jnp.concatenate([got[p, tpo:] for p in range(n)], axis=0).astype(BF)

    run(
        [back]
        + [functools.partial(rs_step, "b", l) for l in range(k - 1)]
        + [cots]
        + [functools.partial(ag_step, "g", "b", l) for l in range(k - 1, 0, -1)]
        + [spread]
    )


def product_kernel(tt_ref, gc_ref, uc_ref, gate_ref, up_ref):
    tt = tt_ref[...]
    gate_ref[...] = jnp.dot(tt, gc_ref[0], preferred_element_type=F32).astype(BF)
    up_ref[...] = jnp.dot(tt, uc_ref[0], preferred_element_type=F32).astype(BF)


def body(n, nr, tokens, gate_weight, up_weight, down_weight, gate_tangent, up_tangent):
    k = n.bit_length() - 1
    depth, units = gate_weight.shape
    total = tokens.shape[0] * nr
    chunk = units // CHUNKS
    half = chunk // 2
    tpo = total // n
    dma = pltpu.SemaphoreType.DMA
    vm = pltpu.VMEM
    scratch = [
        ("x", vm((total, depth), BF)),
        ("w", vm((SLOTS, 4, depth, chunk), BF)),
        ("dn", vm((CHUNKS, chunk, depth), BF)),
        ("pf", vm((4, total, chunk), F32)),
        ("pb", vm((total, chunk), F32)),
        ("h", vm((CHUNKS, n, 2 * tpo, half), BF)),
        ("g", vm((CHUNKS, n, 2 * tpo, chunk), BF)),
        ("cg", vm((CHUNKS, tpo, chunk), F32)),
        ("cu", vm((CHUNKS, tpo, chunk), F32)),
        ("acc", vm((total, depth), F32)),
        ("q", vm((nr, total // nr, depth), BF)),
        ("qs", vm((nr, total // nr, depth), BF)),
        ("o", vm((total, depth), BF)),
        ("wsem", dma((SLOTS, 4))),
        ("dsem", dma((CHUNKS,))),
        ("osem", dma),
    ]
    for tag, rows, cols in (("h", 4 * tpo, chunk), ("b", 2 * tpo, half)):
        for l in range(k):
            shape = (CHUNKS, n >> (l + 1), rows, cols)
            scratch += [
                (tag + "k%d" % l, vm(shape, F32)),
                (tag + "s%d" % l, vm(shape, BF)),
                (tag + "r%d" % l, vm(shape, BF)),
            ]
        scratch += [(tag + e, dma((k, CHUNKS))) for e in ("ss", "rs", "sa", "ra")]
    for tag in "tpo":
        scratch += [(tag + e, dma((nr,))) for e in "sr"]
    names = ["tokens", "gw", "uw", "gt", "ut", "dw", "gc", "uc", "tt"] + [s[0] for s in scratch]
    cot = jax.ShapeDtypeStruct((CHUNKS, total, chunk), BF)
    gate_cot, up_cot, tokens_t = pl.pallas_call(
        functools.partial(curvature_kernel, n, nr, k, names),
        out_shape=(cot, cot, jax.ShapeDtypeStruct((depth, total), BF)),
        in_specs=[pl.BlockSpec(memory_space=pl.ANY)] * 6,
        out_specs=[pl.BlockSpec(memory_space=pltpu.VMEM)] * 3,
        scratch_shapes=[s[1] for s in scratch],
        compiler_params=pltpu.CompilerParams(
            collective_id=0, has_side_effects=True, vmem_limit_bytes=60 * 1024 * 1024
        ),
        name="curvature",
    )(tokens, gate_weight, up_weight, gate_tangent, up_tangent, down_weight)
    product = jax.ShapeDtypeStruct((depth, units), BF)
    return pl.pallas_call(
        product_kernel,
        grid=(CHUNKS,),
        out_shape=(product, product),
        in_specs=[
            pl.BlockSpec((depth, total), lambda c: (0, 0)),
            pl.BlockSpec((1, total, chunk), lambda c: (c, 0, 0)),
            pl.BlockSpec((1, total, chunk), lambda c: (c, 0, 0)),
        ],
        out_specs=[pl.BlockSpec((depth, chunk), lambda c: (0, c))] * 2,
        compiler_params=pltpu.CompilerParams(vmem_limit_bytes=32 * 1024 * 1024),
        name="products",
    )(tokens_t, gate_cot, up_cot)


def solution(mesh):
    placed = (
        P("row", "col"),
        P("col", "row"),
        P("col", "row"),
        P("row", "col"),
        P("col", "row"),
        P("col", "row"),
    )
    return jax.shard_map(
        functools.partial(body, mesh.shape["col"], mesh.shape["row"]),
        mesh=mesh,
        in_specs=placed,
        out_specs=(P("col", "row"), P("col", "row")),
        check_vma=False,
    )
```

time: 333 us -> 128 us (0.38)
  waiting for transfers between devices: 207 us -> 0 us
  Pallas kernels: 0 us -> 124 us
  matrix products: 56.3 us -> 0 us
  local copies, waits for them, and re-layouts: 39.3 us -> 3.25 us
  blocking collectives: 15.3 us -> 0 us
  between operations: 13.8 us -> 0.65 us
    psum x3 -> x0, waiting for transfers between devices: 207 us -> none  [the longest x1 112 us: body(): lax.psum((matmul(gathered, gate_weight), matmul(gathered, up_weight), mat...]
    pallas_call x0 -> x2, Pallas kernels: none -> 124 us  [the longest x1 112 us: body(): pl.pallas_call(functools.partial(curvature_kernel, n, nr, k, names), out_...]
    dot_general x8 -> x0, matrix products: 56.3 us -> none  [the longest x5 30.4 us: matmul(): return jnp.dot(left, right, preferred_element_type=jnp.float32)]
    unnamed x14 -> x6, local copies, waits for them, and re-layouts: 39.3 us -> 3.25 us
    all_gather x1 -> x0, blocking collectives: 15.3 us -> none  [body(): gathered = lax.all_gather(tokens, 'row', axis=0, tiled=True)]
  transfers between devices with their start and end apart: 3 -> 0, of which waited for: 3 -> 0; matrix products, arithmetic and copies ran while one was open for 0% -> 0% of each run, Pallas kernels for 0% -> 0%
where the time goes in v1:
time: 128 us
  Pallas kernels  124 us (97%)
  local copies, waits for them, and re-layouts  3.25 us (3%)
    pallas_call x1, Pallas kernels, body(): pl.pallas_call(functools.partial(curvature_kernel, n, nr, k, names), out_...  112 us
    pallas_call x1, Pallas kernels, body(): pl.pallas_call(product_kernel, grid=(CHUNKS,), out_shape=(product, produc...  11.9 us
    unnamed x6, local copies, waits for them, and re-layouts  3.25 us

profile of v1, /device:TPU:0, one launch (start us, length us, event | category | flops | bytes accessed | tf_op | source)
XLA Modules:
  0.0 127.6 jit_solution(6163516237643874019)
XLA Ops:
  0.6 111.7 %curvature.1 = (bf16[13,64,512]{2,1,0:T(8,128)(2,1)}, bf16[13,64,512]{2,1,0:T(8,128)(2,1)}, bf16[1024,64]{1,0:T(8,128)(2,1)}) custom-call(bf16[16,1024]{1,0:T(8,128)(2,1)} %refs_0_.1, bf16[1024,6656]{1,0:T(8,128)(2,1)} %refs_1_.1, bf16[1024,6656]{1,0:T(8,128)(2,1)} %refs_2_.1, bf16[1024,6656]{1,0:T(8,128)(2,1)} %refs_3_.1, bf16[1024,6656]{1,0:T(8,128)(2,1)} %refs_4_.1, ...), custom_call_target="tpu_custom_call" | custom-call | tf_op jit(solution)/shard_map/curvature/pallas_call | solution.py:322
  112.4 0.0 copy-start
  112.4 1.1 copy-done
  113.5 0.0 copy-start.1
  113.5 1.2 copy-done.1
  114.7 0.0 copy-start.2
  114.7 0.9 copy-done.2
  115.7 11.9 %products.1 = (bf16[1024,6656]{1,0:T(8,128)(2,1)}, bf16[1024,6656]{1,0:T(8,128)(2,1)}) custom-call(bf16[1024,64]{1,0:T(8,128)(2,1)S(1)} %copy-done.2, bf16[13,64,512]{2,1,0:T(8,128)(2,1)S(1)} %copy-done, bf16[13,64,512]{2,1,0:T(8,128)(2,1)S(1)} %copy-done.1), custom_call_target="tpu_custom_call" | custom-call | tf_op jit(solution)/shard_map/products/pallas_call | solution.py:334
Async XLA Ops:
  112.4 1.2 copy-start
  113.5 1.2 copy-start.1
  114.7 0.9 copy-start.2

commit v2 on v1

--- a/solution.py
+++ b/solution.py
@@ -10,9 +10,10 @@
 BF = jnp.bfloat16
 F32 = jnp.float32
 MESH = pl.DeviceIdType.MESH
-SLOTS = 3
+SLOTS = 4
 CHUNKS = 13
-LAG = 1
+HIDDEN_LAG = 2
+BACK_LAG = 3
 
 
 def curvature_kernel(n, nr, k, names, *refs):
@@ -190,24 +191,25 @@
         hid = jnp.concatenate(rows, axis=0).astype(BF)
         r["acc"][...] += jnp.dot(hid, dn[c], preferred_element_type=F32)
 
-    def run(stages):
+    def run(lag, stages):
         def step(i, carry):
             for s, stage in enumerate(stages):
-                c = i - s * LAG
+                c = i - s * lag
 
                 @pl.when(jnp.logical_and(c >= 0, c < CHUNKS))
                 def _():
                     stage(c)
             return carry
 
-        lax.fori_loop(0, CHUNKS + LAG * (len(stages) - 1), step, 0)
+        lax.fori_loop(0, CHUNKS + lag * (len(stages) - 1), step, 0)
 
     run(
+        HIDDEN_LAG,
         [project]
         + [functools.partial(rs_step, "h", l) for l in range(k - 1)]
         + [hidden]
         + [functools.partial(ag_step, "h", "h", l) for l in range(k - 1, 0, -1)]
-        + [down_part]
+        + [down_part],
     )
 
     acc, q, qs, o = r["acc"], r["q"], r["qs"], r["o"]
@@ -265,11 +267,12 @@
         r["uc"][c] = jnp.concatenate([got[p, tpo:] for p in range(n)], axis=0).astype(BF)
 
     run(
+        BACK_LAG,
         [back]
         + [functools.partial(rs_step, "b", l) for l in range(k - 1)]
         + [cots]
         + [functools.partial(ag_step, "g", "b", l) for l in range(k - 1, 0, -1)]
-        + [spread]
+        + [spread],
     )
 
 
@@ -341,7 +344,7 @@
             pl.BlockSpec((1, total, chunk), lambda c: (c, 0, 0)),
         ],
         out_specs=[pl.BlockSpec((depth, chunk), lambda c: (0, c))] * 2,
-        compiler_params=pltpu.CompilerParams(vmem_limit_bytes=32 * 1024 * 1024),
+        compiler_params=pltpu.CompilerParams(vmem_limit_bytes=60 * 1024 * 1024),
         name="products",
     )(tokens_t, gate_cot, up_cot)
 

time: 128 us -> 98.9 us (0.77)
  Pallas kernels: 124 us -> 97.4 us
  local copies, waits for them, and re-layouts: 3.25 us -> 0 us
    pallas_call x1, Pallas kernels: 112 us -> 83.9 us  [body(): pl.pallas_call(functools.partial(curvature_kernel, n, nr, k, names), out_...]
    unnamed x6 -> x0, local copies, waits for them, and re-layouts: 3.25 us -> none
    pallas_call x1, Pallas kernels: 11.9 us -> 13.6 us  [body(): pl.pallas_call(product_kernel, grid=(CHUNKS,), out_shape=(product, produc...]
where the time goes in v2:
time: 98.9 us; the launch traced here: 98.1 us
  Pallas kernels  97.4 us (98%)
    pallas_call x1, Pallas kernels, body(): pl.pallas_call(functools.partial(curvature_kernel, n, nr, k, names), out_...  83.9 us
    pallas_call x1, Pallas kernels, body(): pl.pallas_call(product_kernel, grid=(CHUNKS,), out_shape=(product, produc...  13.6 us

profile of v2, /device:TPU:0, one launch (start us, length us, event | category | flops | bytes accessed | tf_op | source)
XLA Modules:
  0.0 98.1 jit_solution(5253637298873565661)
XLA Ops:
  0.6 83.9 %curvature.1 = (bf16[13,64,512]{2,1,0:T(8,128)(2,1)}, bf16[13,64,512]{2,1,0:T(8,128)(2,1)}, bf16[1024,64]{1,0:T(8,128)(2,1)}) custom-call(bf16[16,1024]{1,0:T(8,128)(2,1)} %refs_0_.1, bf16[1024,6656]{1,0:T(8,128)(2,1)} %refs_1_.1, bf16[1024,6656]{1,0:T(8,128)(2,1)} %refs_2_.1, bf16[1024,6656]{1,0:T(8,128)(2,1)} %refs_3_.1, bf16[1024,6656]{1,0:T(8,128)(2,1)} %refs_4_.1, ...), custom_call_target="tpu_custom_call" | custom-call | tf_op jit(solution)/shard_map/curvature/pallas_call | solution.py:325
  84.5 13.6 %products.1 = (bf16[1024,6656]{1,0:T(8,128)(2,1)}, bf16[1024,6656]{1,0:T(8,128)(2,1)}) custom-call(bf16[1024,64]{1,0:T(8,128)(2,1)} %get-tuple-element.5.tt_ref, bf16[13,64,512]{2,1,0:T(8,128)(2,1)} %get-tuple-element.6.gc_ref, bf16[13,64,512]{2,1,0:T(8,128)(2,1)} %get-tuple-element.7.uc_ref), custom_call_target="tpu_custom_call" | custom-call | tf_op jit(solution)/shard_map/products/pallas_call | solution.py:337

commit v3 on v2

--- a/solution.py
+++ b/solution.py
@@ -13,7 +13,8 @@
 SLOTS = 4
 CHUNKS = 13
 HIDDEN_LAG = 2
-BACK_LAG = 3
+BACK_LAG = 2
+GROUPS = ((0, 2, 4, 6), (1, 3, 5), (8, 10, 12), (7, 9, 11))
 
 
 def curvature_kernel(n, nr, k, names, *refs):
@@ -31,7 +32,8 @@
     def stride(l, c):
         a = 1 << l
         b = 1 if l == 0 else 1 << (k - l)
-        return a if a == b else a + (b - a) * lax.rem(c, 2)
+        odd = c % 2 if isinstance(c, int) else lax.rem(c, 2)
+        return a if a == b else a + (b - a) * odd
 
     def bit(l, c):
         return lax.rem(lax.div(me, stride(l, c)), 2)
@@ -238,42 +240,105 @@
         out_send(d).wait_send()
         out_arrival(d).wait_recv()
 
-    def back(c):
+    starts = [sum(len(g) for g in GROUPS[:i]) for i in range(len(GROUPS))]
+
+    def held(g):
+        return pl.ds(starts[g], len(GROUPS[g]))
+
+    def back_copy(l, g):
+        c = GROUPS[g][0]
+        return pltpu.make_async_remote_copy(
+            src_ref=r["bs%d" % l].at[held(g)],
+            dst_ref=r["br%d" % l].at[held(g)],
+            send_sem=r["bss"].at[l, g],
+            recv_sem=r["brs"].at[l, g],
+            device_id=(row, partner(l, c)),
+            device_id_type=MESH,
+        )
+
+    def cot_copy(l, g, arriving=False):
+        c = GROUPS[g][0]
+        size = 1 << (k - 1 - l)
+        base = lax.div(place(c), size) * size
+        if arriving:
+            base = base + (1 - 2 * bit(l, c)) * size
+        part = r["g"].at[held(g), pl.ds(base, size)]
+        return pltpu.make_async_remote_copy(
+            src_ref=part,
+            dst_ref=part,
+            send_sem=r["bsa"].at[l, g],
+            recv_sem=r["bra"].at[l, g],
+            device_id=(row, partner(l, c)),
+            device_id_type=MESH,
+        )
+
+    def cot_wait(l, g):
+        cot_copy(l, g).wait_send()
+        cot_copy(l, g, arriving=True).wait_recv()
+
+    def back(g):
         pb = r["pb"]
-        pb[...] = lax.dot_general(
-            o[...], dn[c], (((1,), (1,)), ((), ())), preferred_element_type=F32
-        )
-        b = bit(0, c)
+        b = bit(0, 0)
         span = total // 2
-        for p in range(n // 2):
-            rows = pl.ds(pl.multiple_of((1 - b) * span + p * tpo, tpo), tpo)
-            r["bs0"][c, p] = jnp.concatenate([pb[rows, :half], pb[rows, half:]], axis=0).astype(BF)
-        rs_copy("b", 0, c).start()
-        for p in range(n // 2):
-            rows = pl.ds(pl.multiple_of(b * span + p * tpo, tpo), tpo)
-            r["bk0"][c, p] = jnp.concatenate([pb[rows, :half], pb[rows, half:]], axis=0)
-
-    def cots(c):
-        sums = rs_last("b", c)
-        back_sum = jnp.concatenate([sums[:tpo], sums[tpo:]], axis=1)
-        both = [back_sum * r["cg"][c], back_sum * r["cu"][c]]
-        r["g"][c, place(c)] = jnp.concatenate(both, axis=0).astype(BF)
-        ag_copy("g", "b", k - 1, c).start()
-
-    def spread(c):
-        ag_wait("g", "b", 0, c)
-        got = r["g"][c].astype(F32)
-        r["gc"][c] = jnp.concatenate([got[p, :tpo] for p in range(n)], axis=0).astype(BF)
-        r["uc"][c] = jnp.concatenate([got[p, tpo:] for p in range(n)], axis=0).astype(BF)
-
-    run(
-        BACK_LAG,
-        [back]
-        + [functools.partial(rs_step, "b", l) for l in range(k - 1)]
-        + [cots]
-        + [functools.partial(ag_step, "g", "b", l) for l in range(k - 1, 0, -1)]
-        + [spread],
-    )
+        for i, c in enumerate(GROUPS[g]):
+            at = starts[g] + i
+            pb[i] = lax.dot_general(
+                o[...], dn[c], (((1,), (1,)), ((), ())), preferred_element_type=F32
+            )
+            for p in range(n // 2):
+                rows = pl.ds(pl.multiple_of((1 - b) * span + p * tpo, tpo), tpo)
+                both = [pb[i, rows, :half], pb[i, rows, half:]]
+                r["bs0"][at, p] = jnp.concatenate(both, axis=0).astype(BF)
+        back_copy(0, g).start()
+        for i, c in enumerate(GROUPS[g]):
+            at = starts[g] + i
+            for p in range(n // 2):
+                rows = pl.ds(pl.multiple_of(b * span + p * tpo, tpo), tpo)
+                both = [pb[i, rows, :half], pb[i, rows, half:]]
+                r["bk0"][at, p] = jnp.concatenate(both, axis=0)
+
+    def back_step(l, g):
+        back_copy(l, g).wait()
+        kept, got = r["bk%d" % l], r["br%d" % l]
+        m = kept.shape[1] // 2
+        b = bit(l + 1, GROUPS[g][0])
+        other, mine = pl.ds((1 - b) * m, m), pl.ds(b * m, m)
+        at = held(g)
+        r["bs%d" % (l + 1)][at] = (kept[at, other] + got[at, other].astype(F32)).astype(BF)
+        back_copy(l + 1, g).start()
+        r["bk%d" % (l + 1)][at] = kept[at, mine] + got[at, mine].astype(F32)
+
+    def cots(g):
+        back_copy(k - 1, g).wait()
+        for i, c in enumerate(GROUPS[g]):
+            at = starts[g] + i
+            sums = r["bk%d" % (k - 1)][at, 0] + r["br%d" % (k - 1)][at, 0].astype(F32)
+            back_sum = jnp.concatenate([sums[:tpo], sums[tpo:]], axis=1)
+            both = [back_sum * r["cg"][c], back_sum * r["cu"][c]]
+            r["g"][at, place(c)] = jnp.concatenate(both, axis=0).astype(BF)
+        cot_copy(k - 1, g).start()
+
+    def cot_step(l, g):
+        cot_wait(l, g)
+        cot_copy(l - 1, g).start()
+
+    def spread(g):
+        cot_wait(0, g)
+        for i, c in enumerate(GROUPS[g]):
+            got = r["g"][starts[g] + i].astype(F32)
+            r["gc"][c] = jnp.concatenate([got[p, :tpo] for p in range(n)], axis=0).astype(BF)
+            r["uc"][c] = jnp.concatenate([got[p, tpo:] for p in range(n)], axis=0).astype(BF)
+
+    stages = [back]
+    stages += [functools.partial(back_step, l) for l in range(k - 1)]
+    stages += [cots]
+    stages += [functools.partial(cot_step, l) for l in range(k - 1, 0, -1)]
+    stages += [spread]
+    for i in range(len(GROUPS) + BACK_LAG * (len(stages) - 1)):
+        for s, stage in enumerate(stages):
+            g = i - s * BACK_LAG
+            if 0 <= g < len(GROUPS):
+                stage(g)
 
 
 def product_kernel(tt_ref, gc_ref, uc_ref, gate_ref, up_ref):
@@ -296,7 +361,7 @@
         ("w", vm((SLOTS, 4, depth, chunk), BF)),
         ("dn", vm((CHUNKS, chunk, depth), BF)),
         ("pf", vm((4, total, chunk), F32)),
-        ("pb", vm((total, chunk), F32)),
+        ("pb", vm((max(len(g) for g in GROUPS), total, chunk), F32)),
         ("h", vm((CHUNKS, n, 2 * tpo, half), BF)),
         ("g", vm((CHUNKS, n, 2 * tpo, chunk), BF)),
         ("cg", vm((CHUNKS, tpo, chunk), F32)),

time: 98.9 us -> 98 us (level)
  no operation moved by 1% of the time
where the time goes in v3:
time: 98 us; the launch traced here: 97.1 us
  Pallas kernels  96.5 us (98%)
    pallas_call x1, Pallas kernels, body(): pl.pallas_call(functools.partial(curvature_kernel, n, nr, k, names), out_...  82.9 us
    pallas_call x1, Pallas kernels, body(): pl.pallas_call(product_kernel, grid=(CHUNKS,), out_shape=(product, produc...  13.6 us

profile of v3, /device:TPU:0, one launch (start us, length us, event | category | flops | bytes accessed | tf_op | source)
XLA Modules:
  0.0 97.1 jit_solution(8351352532737913593)
XLA Ops:
  0.6 82.9 %curvature.1 = (bf16[13,64,512]{2,1,0:T(8,128)(2,1)}, bf16[13,64,512]{2,1,0:T(8,128)(2,1)}, bf16[1024,64]{1,0:T(8,128)(2,1)}) custom-call(bf16[16,1024]{1,0:T(8,128)(2,1)} %refs_0_.1, bf16[1024,6656]{1,0:T(8,128)(2,1)} %refs_1_.1, bf16[1024,6656]{1,0:T(8,128)(2,1)} %refs_2_.1, bf16[1024,6656]{1,0:T(8,128)(2,1)} %refs_3_.1, bf16[1024,6656]{1,0:T(8,128)(2,1)} %refs_4_.1, ...), custom_call_target="tpu_custom_call" | custom-call | tf_op jit(solution)/shard_map/curvature/pallas_call | solution.py:390
  83.5 13.6 %products.1 = (bf16[1024,6656]{1,0:T(8,128)(2,1)}, bf16[1024,6656]{1,0:T(8,128)(2,1)}) custom-call(bf16[1024,64]{1,0:T(8,128)(2,1)} %get-tuple-element.5.tt_ref, bf16[13,64,512]{2,1,0:T(8,128)(2,1)} %get-tuple-element.6.gc_ref, bf16[13,64,512]{2,1,0:T(8,128)(2,1)} %get-tuple-element.7.uc_ref), custom_call_target="tpu_custom_call" | custom-call | tf_op jit(solution)/shard_map/products/pallas_call | solution.py:402

commit v4 on v3

--- a/solution.py
+++ b/solution.py
@@ -12,7 +12,6 @@
 MESH = pl.DeviceIdType.MESH
 SLOTS = 4
 CHUNKS = 13
-HIDDEN_LAG = 2
 BACK_LAG = 2
 GROUPS = ((0, 2, 4, 6), (1, 3, 5), (8, 10, 12), (7, 9, 11))
 
@@ -193,20 +192,20 @@
         hid = jnp.concatenate(rows, axis=0).astype(BF)
         r["acc"][...] += jnp.dot(hid, dn[c], preferred_element_type=F32)
 
-    def run(lag, stages):
+    def run(lags, stages):
         def step(i, carry):
-            for s, stage in enumerate(stages):
-                c = i - s * lag
+            for lag, stage in zip(lags, stages):
+                c = i - lag
 
                 @pl.when(jnp.logical_and(c >= 0, c < CHUNKS))
                 def _():
                     stage(c)
             return carry
 
-        lax.fori_loop(0, CHUNKS + lag * (len(stages) - 1), step, 0)
+        lax.fori_loop(0, CHUNKS + lags[-1], step, 0)
 
     run(
-        HIDDEN_LAG,
+        [0, 1] + [1 + 2 * l for l in range(1, k)] + [2 * k - 1 + l for l in range(1, k + 1)],
         [project]
         + [functools.partial(rs_step, "h", l) for l in range(k - 1)]
         + [hidden]
@@ -342,9 +341,13 @@
 
 
 def product_kernel(tt_ref, gc_ref, uc_ref, gate_ref, up_ref):
-    tt = tt_ref[...]
-    gate_ref[...] = jnp.dot(tt, gc_ref[0], preferred_element_type=F32).astype(BF)
-    up_ref[...] = jnp.dot(tt, uc_ref[0], preferred_element_type=F32).astype(BF)
+    depth, chunk = gate_ref.shape
+    for cot_ref, out_ref in ((gc_ref, gate_ref), (uc_ref, up_ref)):
+        for col in range(0, chunk, 256):
+            cot = cot_ref[0, :, col:col + 256]
+            for at in range(0, depth, 256):
+                part = jnp.dot(tt_ref[at:at + 256], cot, preferred_element_type=F32)
+                out_ref[at:at + 256, col:col + 256] = part.astype(BF)
 
 
 def body(n, nr, tokens, gate_weight, up_weight, down_weight, gate_tangent, up_tangent):

time: 98 us -> 105 us (1.071)
  Pallas kernels: 96.5 us -> 103 us
    pallas_call x1, Pallas kernels: 82.9 us -> 89.8 us  [body(): pl.pallas_call(functools.partial(curvature_kernel, n, nr, k, names), out_...]
where the time goes in v4:
time: 105 us; the launch traced here: 104 us
  Pallas kernels  103 us (98%)
    pallas_call x1, Pallas kernels, body(): pl.pallas_call(functools.partial(curvature_kernel, n, nr, k, names), out_...  89.8 us
    pallas_call x1, Pallas kernels, body(): pl.pallas_call(product_kernel, grid=(CHUNKS,), out_shape=(product, produc...  13.6 us

profile of v4, /device:TPU:0, one launch (start us, length us, event | category | flops | bytes accessed | tf_op | source)
XLA Modules:
  0.0 104.1 jit_solution(13717979401767018617)
XLA Ops:
  0.6 89.8 %curvature.1 = (bf16[13,64,512]{2,1,0:T(8,128)(2,1)}, bf16[13,64,512]{2,1,0:T(8,128)(2,1)}, bf16[1024,64]{1,0:T(8,128)(2,1)}) custom-call(bf16[16,1024]{1,0:T(8,128)(2,1)} %refs_0_.1, bf16[1024,6656]{1,0:T(8,128)(2,1)} %refs_1_.1, bf16[1024,6656]{1,0:T(8,128)(2,1)} %refs_2_.1, bf16[1024,6656]{1,0:T(8,128)(2,1)} %refs_3_.1, bf16[1024,6656]{1,0:T(8,128)(2,1)} %refs_4_.1, ...), custom_call_target="tpu_custom_call" | custom-call | tf_op jit(solution)/shard_map/curvature/pallas_call | solution.py:393
  90.5 13.6 %products.1 = (bf16[1024,6656]{1,0:T(8,128)(2,1)}, bf16[1024,6656]{1,0:T(8,128)(2,1)}) custom-call(bf16[1024,64]{1,0:T(8,128)(2,1)} %get-tuple-element.5.tt_ref, bf16[13,64,512]{2,1,0:T(8,128)(2,1)} %get-tuple-element.6.gc_ref, bf16[13,64,512]{2,1,0:T(8,128)(2,1)} %get-tuple-element.7.uc_ref), custom_call_target="tpu_custom_call" | custom-call | tf_op jit(solution)/shard_map/products/pallas_call | solution.py:405
